TPU v7x, 128 devices: a whole 4x4x4 slice. The times are simulated.
128 devices in a mesh: slab: 32 (over y, z, x_lo), run: 4 (over x_hi, core).
Axes of the slice: x: 4 (x_hi: 2, x_lo: 2; x = x_hi * 2 + x_lo), y: 4, z: 4, core: 2. Of those that a mesh axis runs over, the one named last changes fastest.
Arguments:
- material: int32 [128, 256, 256], P('slab'), may hold values from 0 to 15
- eps_table: float32 [16], replicated, may hold values from 1 to 12
- surface_mask: int32 [128], P('slab'), may hold values 0 or 1
- excite_map: int32 [4], P('run'), may hold values from 0 to 3
- mode_profiles: float32 [4, 256, 256], P(None, 'slab'), may hold values from -4 to 4
- port_eps: float32 [256, 256], P('slab'), may hold values from 1 to 4
- cotangent: float32 [4, 128, 256, 256], P('run', 'slab'), may hold values from -6 to 6
Outputs:
- gradient: float32 [128, 256, 256], P('slab')
- field_out: float32 [4, 128, 256, 256], P('run', 'slab')
Inputs may be any that keep to these rules, and one draw needn't show every extreme that they name: material indices into the permittivity table. `surface_mask`: 0 or 1 for each x layer. `excite_map`: an index of a mode profile.
All inputs are finite; a program needn't handle non-finite values. No bound on the sum of `surface_mask` on one device may be relied on, other than what follows from the above.
Results may differ from a plain program's by a relative error of at most 0.0001.
Values sent between devices are 32-bit elements; how exact they have to be, the bound alone decides.
A program may use at most 128 MiB of HBM per device.

v0:
```python
import jax
import jax.numpy as jnp
from jax import lax
from jax.sharding import PartitionSpec as P

STEPS = 6
time_step = 0.5


def padded_2(x, sides, width):
    for axis, dim in sides:
        size, length = (lax.axis_size(axis), x.shape[dim])
        up = [(i, (i + 1) % size) for i in range(size - 1)]
        down = [(j, i) for i, j in up]
        last = lax.slice_in_dim(x, length - width, length, axis=dim)
        first = lax.slice_in_dim(x, 0, width, axis=dim)
        before = lax.ppermute(last, axis, up)
        after = lax.ppermute(first, axis, down)
        x = jnp.concatenate([before, x, after], axis=dim)
    return x


def passed_along(block, axis, distance):
    devices = range(lax.axis_size(axis))
    route = [(i - distance, i) for i in devices if i - distance in devices]
    return lax.ppermute(block, axis, route)


def rim_zero(field, along):
    return jnp.zeros_like(lax.slice_in_dim(field, 0, 1, axis=along))


def ahead(field, along, border):
    length = field.shape[along]
    return jnp.concatenate([lax.slice_in_dim(field, 1, length, axis=along), border], along) - field


def behind(field, along, border):
    length = field.shape[along]
    return field - jnp.concatenate(
        [border, lax.slice_in_dim(field, 0, length - 1, axis=along)], along
    )


def update_magnetic(electric, magnetic, upper_y, upper_z):
    electric_x, electric_y, electric_z = electric
    magnetic_x, magnetic_y, magnetic_z = magnetic
    magnetic_x = magnetic_x - time_step * (
        ahead(electric_z, 2, rim_zero(electric_z, 2))
        - ahead(electric_y, 3, rim_zero(electric_y, 3))
    )
    magnetic_y = magnetic_y - time_step * (
        ahead(electric_x, 3, rim_zero(electric_x, 3)) - ahead(electric_z, 1, upper_z)
    )
    magnetic_z = magnetic_z - time_step * (
        ahead(electric_y, 1, upper_y) - ahead(electric_x, 2, rim_zero(electric_x, 2))
    )
    return (magnetic_x, magnetic_y, magnetic_z)


def update_electric(electric, magnetic, lower_y, lower_z, coefficient, source_y, source_z):
    electric_x, electric_y, electric_z = electric
    magnetic_x, magnetic_y, magnetic_z = magnetic
    electric_x = electric_x + coefficient * (
        behind(magnetic_z, 2, rim_zero(magnetic_z, 2))
        - behind(magnetic_y, 3, rim_zero(magnetic_y, 3))
    )
    electric_y = (
        electric_y
        + coefficient
        * (behind(magnetic_x, 3, rim_zero(magnetic_x, 3)) - behind(magnetic_z, 1, lower_z))
        + source_y
    )
    electric_z = (
        electric_z
        + coefficient
        * (behind(magnetic_y, 1, lower_y) - behind(magnetic_x, 2, rim_zero(magnetic_x, 2)))
        + source_z
    )
    return (electric_x, electric_y, electric_z)


def modal_advance(modal_now, modal_old, padded, port_coefficient, profile, forcing):
    middle = padded[1:-1]
    zpadded = jnp.pad(middle, ((0, 0), (1, 1)))
    laplacian = padded[2:] + padded[:-2] + zpadded[:, 2:] + zpadded[:, :-2] - 4.0 * middle
    return 2.0 * modal_now - modal_old + port_coefficient * laplacian + forcing * profile


def forcing_at(counter):
    moment = (counter + 1).astype(jnp.float32)
    return 2.0 * jnp.sin(0.3 * moment) * (1.0 - jnp.exp(-0.5 * moment))


def permittivity_of(material, eps_table):
    levels = jnp.arange(eps_table.shape[0], dtype=jnp.int32)
    picked = (material[None] == levels[:, None, None, None]).astype(jnp.float32)
    return jnp.sum(picked * eps_table[:, None, None, None], axis=0)


def local(material, eps_table, surface_mask, excite_map, mode_profiles, port_eps, cotangent):
    coefficient = time_step / permittivity_of(material, eps_table)
    mask_column = surface_mask.astype(jnp.float32)[:, None, None]
    injection = 0.25 * coefficient * mask_column
    selector = jnp.array([1.0, 0.0], jnp.float32)[:, None, None, None]
    choose = (jnp.arange(mode_profiles.shape[0], dtype=jnp.int32) == excite_map[0]).astype(
        jnp.float32
    )
    profile = jnp.sum(mode_profiles * choose[:, None, None], axis=0)
    port_coefficient = 0.25 / port_eps

    def port_step(modal_now, modal_old, forcing):
        padded = padded_2(modal_now, (("slab", 0),), 1)
        modal_next = modal_advance(modal_now, modal_old, padded, port_coefficient, profile, forcing)
        incident_e, incident_h = (
            lax.all_gather(modal_next, "slab", axis=0, tiled=True),
            lax.all_gather(modal_next - modal_now, "slab", axis=0, tiled=True),
        )
        return (modal_next, incident_e, incident_h)

    zeros = jnp.zeros((2,) + coefficient.shape, jnp.float32)
    electric = (zeros.at[0].set(cotangent[0]), zeros, zeros.at[1].set(cotangent[0]))
    magnetic = (zeros, zeros, zeros)
    modal_zero = jnp.zeros_like(profile)

    def advance(counter, carried):
        electric, magnetic, modal_now, modal_old, gradient_sum = carried
        modal_next, incident_e, incident_h = port_step(modal_now, modal_old, forcing_at(counter))
        electric_x, electric_y, electric_z = electric
        upper_rim = passed_along(
            jnp.concatenate([electric_y[:, 0:1], electric_z[:, 0:1]], 1), "slab", -1
        )
        magnetic = update_magnetic(electric, magnetic, upper_rim[:, 0:1], upper_rim[:, 1:2])
        lower_rim = passed_along(
            jnp.concatenate([magnetic[1][:, -1:], magnetic[2][:, -1:]], 1), "slab", 1
        )
        lower_y = lower_rim[:, 0:1]
        lower_z = lower_rim[:, 1:2]
        electric = update_electric(
            electric,
            magnetic,
            lower_y,
            lower_z,
            coefficient,
            selector * (injection * incident_h),
            selector * (injection * incident_e),
        )
        gradient_sum = gradient_sum + (
            electric[0][0] * electric[0][1]
            + electric[1][0] * electric[1][1]
            + electric[2][0] * electric[2][1]
        )
        return (electric, magnetic, modal_next, modal_now, gradient_sum)

    carried = lax.fori_loop(
        0,
        STEPS,
        advance,
        (electric, magnetic, modal_zero, modal_zero, jnp.zeros(coefficient.shape, jnp.float32)),
    )
    gradient = lax.psum(carried[4], "run")
    return (gradient, carried[0][1][0][None])


def solution(mesh):
    in_specs = (
        P("slab", None, None),
        P(),
        P("slab"),
        P("run"),
        P(None, "slab", None),
        P("slab", None),
        P("run", "slab", None, None),
    )
    out_specs = (P("slab", None, None), P("run", "slab", None, None))
    return jax.shard_map(local, mesh=mesh, in_specs=in_specs, out_specs=out_specs, check_vma=False)
```

profile of v0, /device:TPU:1, one launch (start us, length us, event | category | flops | bytes accessed | tf_op | source)
XLA Modules:
  0.0 1372.4 jit_solution(14720914317729965856)
XLA Ops:
  7.3 3.4 fusion.32
  14.8 1125.8 %while.35 = (s32[]{:T(128)}, f32[2,4,256,256]{3,2,1,0:T(8,128)S(1)}, f32[2,4,256,256]{3,2,1,0:T(8,128)}, f32[2,4,256,256]{3,2,1,0:T(8,128)}, f32[2,4,256,256]{3,...) while((s32[]{:T(128)}, ...), condition=%wide.region_3.0_spmd.clone.clone, body=%wide.region_2.0_spmd.clone.clone.sunk | while | flops 25982984 | bytes 269106240 | solution.py:155
  15.1 2.1 copy-done
  20.4 23.2 %collective-permute-done = f32[2,2,256,256]{3,2,1,0:T(8,128)S(1)} collective-permute-done((f32[2,2,256,256]{3,2,1,0:T(8,128)S(1)}, f32[2,2,256,256]{3,2,1,0:T(8,128)S(1)}, u32[]{:S(2)}, u32[]{:S(2)}) %collective-permute-start) | collective-permute-done | bytes 1048608 | tf_op jit(solution)/shard_map/while/body/eval_jaxpr/ppermute | solution.py:26
  43.7 2.2 select_subtract_fusion.2
  48.2 5.4 collective-permute-start.1
  56.7 17.1 %collective-permute-done.2 = f32[1,256]{1,0:T(1,128)S(1)} collective-permute-done((f32[1,256]{1,0:T(1,128)S(1)}, f32[1,256]{1,0:T(1,128)S(1)}, u32[]{:S(2)}, u32[]{:S(2)}) %collective-permute-start.2) | collective-permute-done | bytes 1056 | tf_op jit(solution)/shard_map/while/body/eval_jaxpr/ppermute | solution.py:17
  75.6 69.1 %all_gather.26 = f32[256,256]{1,0:T(8,128)S(1)} all-gather(f32[8,256]{1,0:T(8,128)S(1)} %get-tuple-element.732), channel_id=1, replica_groups=mesh['slab'=32,'run'=4] {'slab'}, dimensions={0}, use_global_device_ids=true | all-gather | bytes 270336 | tf_op jit(solution)/shard_map/while/body/eval_jaxpr/all_gather | solution.py:116
  144.7 63.4 %all_gather.27 = f32[256,256]{1,0:T(8,128)S(1)} all-gather(f32[8,256]{1,0:T(8,128)S(1)} %get-tuple-element.676), channel_id=1, replica_groups=mesh['slab'=32,'run'=4] {'slab'}, dimensions={0}, use_global_device_ids=true | all-gather | bytes 270336 | tf_op jit(solution)/shard_map/while/body/eval_jaxpr/all_gather | solution.py:117
  210.2 2.6 fusion.40
  213.1 5.3 fusion.43
  220.8 2.0 broadcast_select_fusion.4
  226.3 12.8 collective-permute-done
  239.2 2.2 select_subtract_fusion.2
  243.7 5.1 collective-permute-start.1
  251.5 8.3 collective-permute-done.2
  259.8 2.7 collective-permute-done.3
  263.2 63.8 %all_gather.26 = f32[256,256]{1,0:T(8,128)S(1)} all-gather(f32[8,256]{1,0:T(8,128)S(1)} %get-tuple-element.732), channel_id=1, replica_groups=mesh['slab'=32,'run'=4] {'slab'}, dimensions={0}, use_global_device_ids=true | all-gather | bytes 270336 | tf_op jit(solution)/shard_map/while/body/eval_jaxpr/all_gather | solution.py:116
  327.0 65.1 %all_gather.27 = f32[256,256]{1,0:T(8,128)S(1)} all-gather(f32[8,256]{1,0:T(8,128)S(1)} %get-tuple-element.676), channel_id=1, replica_groups=mesh['slab'=32,'run'=4] {'slab'}, dimensions={0}, use_global_device_ids=true | all-gather | bytes 270336 | tf_op jit(solution)/shard_map/while/body/eval_jaxpr/all_gather | solution.py:117
  394.2 2.6 fusion.40
  397.1 5.3 fusion.43
  402.4 3.6 fusion.44
  406.1 2.0 broadcast_select_fusion.4
  411.6 12.7 collective-permute-done
  424.5 2.2 select_subtract_fusion.2
  429.0 3.6 collective-permute-start.1
  435.3 8.9 collective-permute-done.2
  445.4 65.4 %all_gather.26 = f32[256,256]{1,0:T(8,128)S(1)} all-gather(f32[8,256]{1,0:T(8,128)S(1)} %get-tuple-element.732), channel_id=1, replica_groups=mesh['slab'=32,'run'=4] {'slab'}, dimensions={0}, use_global_device_ids=true | all-gather | bytes 270336 | tf_op jit(solution)/shard_map/while/body/eval_jaxpr/all_gather | solution.py:116
  510.8 63.5 %all_gather.27 = f32[256,256]{1,0:T(8,128)S(1)} all-gather(f32[8,256]{1,0:T(8,128)S(1)} %get-tuple-element.676), channel_id=1, replica_groups=mesh['slab'=32,'run'=4] {'slab'}, dimensions={0}, use_global_device_ids=true | all-gather | bytes 270336 | tf_op jit(solution)/shard_map/while/body/eval_jaxpr/all_gather | solution.py:117
  576.4 2.6 fusion.40
  579.3 5.3 fusion.43
  584.6 3.6 fusion.44
  588.3 2.0 broadcast_select_fusion.4
  593.8 13.2 collective-permute-done
  607.1 2.2 select_subtract_fusion.2
  611.6 5.1 collective-permute-start.1
  619.5 8.9 collective-permute-done.2
  629.2 65.6 %all_gather.26 = f32[256,256]{1,0:T(8,128)S(1)} all-gather(f32[8,256]{1,0:T(8,128)S(1)} %get-tuple-element.732), channel_id=1, replica_groups=mesh['slab'=32,'run'=4] {'slab'}, dimensions={0}, use_global_device_ids=true | all-gather | bytes 270336 | tf_op jit(solution)/shard_map/while/body/eval_jaxpr/all_gather | solution.py:116
  694.9 64.3 %all_gather.27 = f32[256,256]{1,0:T(8,128)S(1)} all-gather(f32[8,256]{1,0:T(8,128)S(1)} %get-tuple-element.676), channel_id=1, replica_groups=mesh['slab'=32,'run'=4] {'slab'}, dimensions={0}, use_global_device_ids=true | all-gather | bytes 270336 | tf_op jit(solution)/shard_map/while/body/eval_jaxpr/all_gather | solution.py:117
  761.3 2.6 fusion.40
  764.2 5.3 fusion.43
  769.5 3.6 fusion.44
  773.2 2.0 broadcast_select_fusion.4
  778.7 13.0 collective-permute-done
  791.8 2.2 select_subtract_fusion.2
  796.4 4.6 collective-permute-start.1
  803.7 8.7 collective-permute-done.2
  813.4 65.3 %all_gather.26 = f32[256,256]{1,0:T(8,128)S(1)} all-gather(f32[8,256]{1,0:T(8,128)S(1)} %get-tuple-element.732), channel_id=1, replica_groups=mesh['slab'=32,'run'=4] {'slab'}, dimensions={0}, use_global_device_ids=true | all-gather | bytes 270336 | tf_op jit(solution)/shard_map/while/body/eval_jaxpr/all_gather | solution.py:116
  878.8 64.0 %all_gather.27 = f32[256,256]{1,0:T(8,128)S(1)} all-gather(f32[8,256]{1,0:T(8,128)S(1)} %get-tuple-element.676), channel_id=1, replica_groups=mesh['slab'=32,'run'=4] {'slab'}, dimensions={0}, use_global_device_ids=true | all-gather | bytes 270336 | tf_op jit(solution)/shard_map/while/body/eval_jaxpr/all_gather | solution.py:117
  944.9 2.6 fusion.40
  947.8 5.3 fusion.43
  953.1 3.6 fusion.44
  962.3 12.9 collective-permute-done
  975.3 2.2 select_subtract_fusion.2
  979.8 5.1 collective-permute-start.1
  987.6 8.8 collective-permute-done.2
  997.6 65.0 %all_gather.26 = f32[256,256]{1,0:T(8,128)S(1)} all-gather(f32[8,256]{1,0:T(8,128)S(1)} %get-tuple-element.732), channel_id=1, replica_groups=mesh['slab'=32,'run'=4] {'slab'}, dimensions={0}, use_global_device_ids=true | all-gather | bytes 270336 | tf_op jit(solution)/shard_map/while/body/eval_jaxpr/all_gather | solution.py:116
  1062.7 63.9 %all_gather.27 = f32[256,256]{1,0:T(8,128)S(1)} all-gather(f32[8,256]{1,0:T(8,128)S(1)} %get-tuple-element.676), channel_id=1, replica_groups=mesh['slab'=32,'run'=4] {'slab'}, dimensions={0}, use_global_device_ids=true | all-gather | bytes 270336 | tf_op jit(solution)/shard_map/while/body/eval_jaxpr/all_gather | solution.py:117
  1128.7 2.6 fusion.40
  1131.6 5.3 fusion.43
  1136.9 3.6 fusion.44
  1140.6 2.3 slice.373
  1142.9 220.3 %all-reduce.13.cloned.1.call-done = f32[4,256,256]{2,1,0:T(8,128)} async-done(((f32[4,256,256]{2,1,0:T(8,128)}), f32[4,256,256]{2,1,0:T(8,128)}) %all-reduce.13.cloned.1.call-update) | async-done | bytes 1048592 | tf_op jit(solution)/shard_map/psum | solution.py:161
  1363.2 2.3 copy.42
  (436 shorter events, 79.6 us)
Async XLA Ops:
  7.2 1356.1 %all-reduce.13.cloned.1.call-start = ((), (), s32[]{:S(2)}) async-start(), calls=%async_computation | async-start | bytes 2097152 | tf_op jit(solution)/shard_map/psum | solution.py:161
  14.8 60.2 %copy-start.17 = (f32[8,256]{1,0:T(8,128)}, f32[8,256]{1,0:T(8,128)S(1)}, u32[]{:S(2)}) copy-start(f32[8,256]{1,0:T(8,128)S(1)} %get-tuple-element.736) | copy-start | bytes 24580 | tf_op jit(solution)/shard_map/while
  14.8 60.2 %copy-start.20 = (f32[8,256]{1,0:T(8,128)}, f32[8,256]{1,0:T(8,128)S(1)}, u32[]{:S(2)}) copy-start(f32[8,256]{1,0:T(8,128)S(1)} %get-tuple-element.737) | copy-start | bytes 24580 | tf_op jit(solution)/shard_map/while
  17.2 26.3 %collective-permute-start = (f32[2,2,256,256]{3,2,1,0:T(8,128)S(1)}, f32[2,2,256,256]{3,2,1,0:T(8,128)S(1)}, u32[]{:S(2)}, u32[]{:S(2)}) collective-permute-start(f32[2,2,256,256]{3,2,1,0:T(8,128)S(1)} %pad_maximum_fusion.6), channel_id=1, source_target_pairs={{4,0},{8,4},{12,8},{16,12},{20,16},{24,20},{28,24},{32,28},{36,32}... | collective-permute-start | bytes 3145736 | tf_op jit(solution)/shard_map/while/body/eval_jaxpr/ppermute | solution.py:26
  19.6 24.1 %copy-start.12 = (f32[2,4,256,256]{3,2,1,0:T(8,128)S(1)}, f32[2,4,256,256]{3,2,1,0:T(8,128)}, u32[]{:S(2)}) copy-start(f32[2,4,256,256]{3,2,1,0:T(8,128)} %get-tuple-element.710) | copy-start | bytes 6291460 | tf_op jit(solution)/shard_map/while
  19.6 24.1 %slice-start = ((f32[2,4,256,256]{3,2,1,0:T(8,128)}), f32[2,3,256,256]{3,2,1,0:T(8,128)S(1)}, s32[]{:S(2)}) async-start(f32[2,4,256,256]{3,2,1,0:T(8,128)} %copy-done.15), calls=%async_computation.1 | async-start | bytes 3145728 | tf_op jit(solution)/shard_map/while/body/eval_jaxpr/slice | solution.py:35
  20.2 23.5 %copy-start.6 = (f32[2,4,256,256]{3,2,1,0:T(8,128)S(1)}, f32[2,4,256,256]{3,2,1,0:T(8,128)}, u32[]{:S(2)}) copy-start(f32[2,4,256,256]{3,2,1,0:T(8,128)} %get-tuple-element.708) | copy-start | bytes 6291460 | tf_op jit(solution)/shard_map/while
  20.2 23.5 %copy-start.9 = (f32[2,4,256,256]{3,2,1,0:T(8,128)S(1)}, f32[2,4,256,256]{3,2,1,0:T(8,128)}, u32[]{:S(2)}) copy-start(f32[2,4,256,256]{3,2,1,0:T(8,128)} %get-tuple-element.709) | copy-start | bytes 6291460 | tf_op jit(solution)/shard_map/while
  20.4 23.3 %copy-start.3 = (f32[2,4,256,256]{3,2,1,0:T(8,128)S(1)}, f32[2,4,256,256]{3,2,1,0:T(8,128)}, u32[]{:S(2)}) copy-start(f32[2,4,256,256]{3,2,1,0:T(8,128)} %get-tuple-element.706) | copy-start | bytes 6291460 | tf_op jit(solution)/shard_map/while
  48.2 162.0 %collective-permute-start.1 = (f32[2,2,256,256]{3,2,1,0:T(8,128)}, f32[2,2,256,256]{3,2,1,0:T(8,128)}, u32[]{:S(2)}, u32[]{:S(2)}) collective-permute-start(f32[2,2,256,256]{3,2,1,0:T(8,128)} %pad_maximum_fusion.7), channel_id=1, source_target_pairs={{0,4},{4,8},{8,12},{12,16},{16,20},{20,24},{24,28},{28,32},{32,36}... | collective-permute-start | bytes 3145736 | tf_op jit(solution)/shard_map/while/body/eval_jaxpr/ppermute | solution.py:26
  53.6 20.2 %collective-permute-start.2 = (f32[1,256]{1,0:T(1,128)S(1)}, f32[1,256]{1,0:T(1,128)S(1)}, u32[]{:S(2)}, u32[]{:S(2)}) collective-permute-start(f32[1,256]{1,0:T(1,128)S(1)} %get-tuple-element.673), channel_id=1, source_target_pairs={{0,4},{4,8},{8,12},{12,16},{16,20},{20,24},{24,28},{28,32},{32,36}... | collective-permute-start | bytes 3080 | tf_op jit(solution)/shard_map/while/body/eval_jaxpr/ppermute | solution.py:17
  55.3 19.6 %collective-permute-start.3 = (f32[1,256]{1,0:T(1,128)S(1)}, f32[1,256]{1,0:T(1,128)S(1)}, u32[]{:S(2)}, u32[]{:S(2)}) collective-permute-start(f32[1,256]{1,0:T(1,128)S(1)} %get-tuple-element.674), channel_id=1, source_target_pairs={{4,0},{8,4},{12,8},{16,12},{20,16},{24,20},{28,24},{32,28},{36,32}... | collective-permute-start | bytes 3080 | tf_op jit(solution)/shard_map/while/body/eval_jaxpr/ppermute | solution.py:18
  75.6 134.0 %copy-start.11 = (f32[2,4,256,256]{3,2,1,0:T(8,128)S(1)}, f32[2,4,256,256]{3,2,1,0:T(8,128)}, u32[]{:S(2)}) copy-start(f32[2,4,256,256]{3,2,1,0:T(8,128)} %copy-done.10) | copy-start | bytes 6291460 | tf_op jit(solution)/shard_map/while
  220.7 41.8 %copy-start.17 = (f32[8,256]{1,0:T(8,128)}, f32[8,256]{1,0:T(8,128)S(1)}, u32[]{:S(2)}) copy-start(f32[8,256]{1,0:T(8,128)S(1)} %get-tuple-element.736) | copy-start | bytes 24580 | tf_op jit(solution)/shard_map/while
  220.7 41.8 %copy-start.20 = (f32[8,256]{1,0:T(8,128)}, f32[8,256]{1,0:T(8,128)S(1)}, u32[]{:S(2)}) copy-start(f32[8,256]{1,0:T(8,128)S(1)} %get-tuple-element.737) | copy-start | bytes 24580 | tf_op jit(solution)/shard_map/while
  223.1 16.0 %collective-permute-start = (f32[2,2,256,256]{3,2,1,0:T(8,128)S(1)}, f32[2,2,256,256]{3,2,1,0:T(8,128)S(1)}, u32[]{:S(2)}, u32[]{:S(2)}) collective-permute-start(f32[2,2,256,256]{3,2,1,0:T(8,128)S(1)} %pad_maximum_fusion.6), channel_id=1, source_target_pairs={{4,0},{8,4},{12,8},{16,12},{20,16},{24,20},{28,24},{32,28},{36,32}... | collective-permute-start | bytes 3145736 | tf_op jit(solution)/shard_map/while/body/eval_jaxpr/ppermute | solution.py:26
  225.4 13.7 %copy-start.12 = (f32[2,4,256,256]{3,2,1,0:T(8,128)S(1)}, f32[2,4,256,256]{3,2,1,0:T(8,128)}, u32[]{:S(2)}) copy-start(f32[2,4,256,256]{3,2,1,0:T(8,128)} %get-tuple-element.710) | copy-start | bytes 6291460 | tf_op jit(solution)/shard_map/while
  225.4 13.7 %slice-start = ((f32[2,4,256,256]{3,2,1,0:T(8,128)}), f32[2,3,256,256]{3,2,1,0:T(8,128)S(1)}, s32[]{:S(2)}) async-start(f32[2,4,256,256]{3,2,1,0:T(8,128)} %copy-done.15), calls=%async_computation.1 | async-start | bytes 3145728 | tf_op jit(solution)/shard_map/while/body/eval_jaxpr/slice | solution.py:35
  243.7 150.5 %collective-permute-start.1 = (f32[2,2,256,256]{3,2,1,0:T(8,128)}, f32[2,2,256,256]{3,2,1,0:T(8,128)}, u32[]{:S(2)}, u32[]{:S(2)}) collective-permute-start(f32[2,2,256,256]{3,2,1,0:T(8,128)} %pad_maximum_fusion.7), channel_id=1, source_target_pairs={{0,4},{4,8},{8,12},{12,16},{16,20},{20,24},{24,28},{28,32},{32,36}... | collective-permute-start | bytes 3145736 | tf_op jit(solution)/shard_map/while/body/eval_jaxpr/ppermute | solution.py:26
  248.8 11.1 collective-permute-start.2
  250.1 12.5 collective-permute-start.3
  263.2 130.5 %copy-start.11 = (f32[2,4,256,256]{3,2,1,0:T(8,128)S(1)}, f32[2,4,256,256]{3,2,1,0:T(8,128)}, u32[]{:S(2)}) copy-start(f32[2,4,256,256]{3,2,1,0:T(8,128)} %copy-done.10) | copy-start | bytes 6291460 | tf_op jit(solution)/shard_map/while
  406.1 38.6 %copy-start.17 = (f32[8,256]{1,0:T(8,128)}, f32[8,256]{1,0:T(8,128)S(1)}, u32[]{:S(2)}) copy-start(f32[8,256]{1,0:T(8,128)S(1)} %get-tuple-element.736) | copy-start | bytes 24580 | tf_op jit(solution)/shard_map/while
  406.1 38.6 %copy-start.20 = (f32[8,256]{1,0:T(8,128)}, f32[8,256]{1,0:T(8,128)S(1)}, u32[]{:S(2)}) copy-start(f32[8,256]{1,0:T(8,128)S(1)} %get-tuple-element.737) | copy-start | bytes 24580 | tf_op jit(solution)/shard_map/while
  408.5 15.9 %collective-permute-start = (f32[2,2,256,256]{3,2,1,0:T(8,128)S(1)}, f32[2,2,256,256]{3,2,1,0:T(8,128)S(1)}, u32[]{:S(2)}, u32[]{:S(2)}) collective-permute-start(f32[2,2,256,256]{3,2,1,0:T(8,128)S(1)} %pad_maximum_fusion.6), channel_id=1, source_target_pairs={{4,0},{8,4},{12,8},{16,12},{20,16},{24,20},{28,24},{32,28},{36,32}... | collective-permute-start | bytes 3145736 | tf_op jit(solution)/shard_map/while/body/eval_jaxpr/ppermute | solution.py:26
  410.8 13.7 copy-start.12
  410.8 13.7 slice-start
  429.0 147.4 %collective-permute-start.1 = (f32[2,2,256,256]{3,2,1,0:T(8,128)}, f32[2,2,256,256]{3,2,1,0:T(8,128)}, u32[]{:S(2)}, u32[]{:S(2)}) collective-permute-start(f32[2,2,256,256]{3,2,1,0:T(8,128)} %pad_maximum_fusion.7), channel_id=1, source_target_pairs={{0,4},{4,8},{8,12},{12,16},{16,20},{20,24},{24,28},{28,32},{32,36}... | collective-permute-start | bytes 3145736 | tf_op jit(solution)/shard_map/while/body/eval_jaxpr/ppermute | solution.py:26
  432.6 11.6 collective-permute-start.2
  433.9 10.8 collective-permute-start.3
  445.4 130.4 %copy-start.11 = (f32[2,4,256,256]{3,2,1,0:T(8,128)S(1)}, f32[2,4,256,256]{3,2,1,0:T(8,128)}, u32[]{:S(2)}) copy-start(f32[2,4,256,256]{3,2,1,0:T(8,128)} %copy-done.10) | copy-start | bytes 6291460 | tf_op jit(solution)/shard_map/while
  588.3 40.3 %copy-start.17 = (f32[8,256]{1,0:T(8,128)}, f32[8,256]{1,0:T(8,128)S(1)}, u32[]{:S(2)}) copy-start(f32[8,256]{1,0:T(8,128)S(1)} %get-tuple-element.736) | copy-start | bytes 24580 | tf_op jit(solution)/shard_map/while
  588.3 40.3 %copy-start.20 = (f32[8,256]{1,0:T(8,128)}, f32[8,256]{1,0:T(8,128)S(1)}, u32[]{:S(2)}) copy-start(f32[8,256]{1,0:T(8,128)S(1)} %get-tuple-element.737) | copy-start | bytes 24580 | tf_op jit(solution)/shard_map/while
  590.6 16.4 %collective-permute-start = (f32[2,2,256,256]{3,2,1,0:T(8,128)S(1)}, f32[2,2,256,256]{3,2,1,0:T(8,128)S(1)}, u32[]{:S(2)}, u32[]{:S(2)}) collective-permute-start(f32[2,2,256,256]{3,2,1,0:T(8,128)S(1)} %pad_maximum_fusion.6), channel_id=1, source_target_pairs={{4,0},{8,4},{12,8},{16,12},{20,16},{24,20},{28,24},{32,28},{36,32}... | collective-permute-start | bytes 3145736 | tf_op jit(solution)/shard_map/while/body/eval_jaxpr/ppermute | solution.py:26
  592.9 14.1 %copy-start.12 = (f32[2,4,256,256]{3,2,1,0:T(8,128)S(1)}, f32[2,4,256,256]{3,2,1,0:T(8,128)}, u32[]{:S(2)}) copy-start(f32[2,4,256,256]{3,2,1,0:T(8,128)} %get-tuple-element.710) | copy-start | bytes 6291460 | tf_op jit(solution)/shard_map/while
  593.0 14.1 %slice-start = ((f32[2,4,256,256]{3,2,1,0:T(8,128)}), f32[2,3,256,256]{3,2,1,0:T(8,128)S(1)}, s32[]{:S(2)}) async-start(f32[2,4,256,256]{3,2,1,0:T(8,128)} %copy-done.15), calls=%async_computation.1 | async-start | bytes 3145728 | tf_op jit(solution)/shard_map/while/body/eval_jaxpr/slice | solution.py:35
  593.6 13.5 copy-start.6
  593.6 13.5 copy-start.9
  593.8 13.3 copy-start.3
  611.6 149.6 %collective-permute-start.1 = (f32[2,2,256,256]{3,2,1,0:T(8,128)}, f32[2,2,256,256]{3,2,1,0:T(8,128)}, u32[]{:S(2)}, u32[]{:S(2)}) collective-permute-start(f32[2,2,256,256]{3,2,1,0:T(8,128)} %pad_maximum_fusion.7), channel_id=1, source_target_pairs={{0,4},{4,8},{8,12},{12,16},{16,20},{20,24},{24,28},{28,32},{32,36}... | collective-permute-start | bytes 3145736 | tf_op jit(solution)/shard_map/while/body/eval_jaxpr/ppermute | solution.py:26
  616.8 11.6 collective-permute-start.2
  618.1 10.5 collective-permute-start.3
  629.2 131.5 %copy-start.11 = (f32[2,4,256,256]{3,2,1,0:T(8,128)S(1)}, f32[2,4,256,256]{3,2,1,0:T(8,128)}, u32[]{:S(2)}) copy-start(f32[2,4,256,256]{3,2,1,0:T(8,128)} %copy-done.10) | copy-start | bytes 6291460 | tf_op jit(solution)/shard_map/while
  773.2 39.6 %copy-start.17 = (f32[8,256]{1,0:T(8,128)}, f32[8,256]{1,0:T(8,128)S(1)}, u32[]{:S(2)}) copy-start(f32[8,256]{1,0:T(8,128)S(1)} %get-tuple-element.736) | copy-start | bytes 24580 | tf_op jit(solution)/shard_map/while
  773.2 39.6 %copy-start.20 = (f32[8,256]{1,0:T(8,128)}, f32[8,256]{1,0:T(8,128)S(1)}, u32[]{:S(2)}) copy-start(f32[8,256]{1,0:T(8,128)S(1)} %get-tuple-element.737) | copy-start | bytes 24580 | tf_op jit(solution)/shard_map/while
  775.5 16.2 %collective-permute-start = (f32[2,2,256,256]{3,2,1,0:T(8,128)S(1)}, f32[2,2,256,256]{3,2,1,0:T(8,128)S(1)}, u32[]{:S(2)}, u32[]{:S(2)}) collective-permute-start(f32[2,2,256,256]{3,2,1,0:T(8,128)S(1)} %pad_maximum_fusion.6), channel_id=1, source_target_pairs={{4,0},{8,4},{12,8},{16,12},{20,16},{24,20},{28,24},{32,28},{36,32}... | collective-permute-start | bytes 3145736 | tf_op jit(solution)/shard_map/while/body/eval_jaxpr/ppermute | solution.py:26
  777.8 14.0 %copy-start.12 = (f32[2,4,256,256]{3,2,1,0:T(8,128)S(1)}, f32[2,4,256,256]{3,2,1,0:T(8,128)}, u32[]{:S(2)}) copy-start(f32[2,4,256,256]{3,2,1,0:T(8,128)} %get-tuple-element.710) | copy-start | bytes 6291460 | tf_op jit(solution)/shard_map/while
  777.9 14.0 %slice-start = ((f32[2,4,256,256]{3,2,1,0:T(8,128)}), f32[2,3,256,256]{3,2,1,0:T(8,128)S(1)}, s32[]{:S(2)}) async-start(f32[2,4,256,256]{3,2,1,0:T(8,128)} %copy-done.15), calls=%async_computation.1 | async-start | bytes 3145728 | tf_op jit(solution)/shard_map/while/body/eval_jaxpr/slice | solution.py:35
  778.5 13.3 copy-start.6
  778.5 13.3 copy-start.9
  796.4 148.5 %collective-permute-start.1 = (f32[2,2,256,256]{3,2,1,0:T(8,128)}, f32[2,2,256,256]{3,2,1,0:T(8,128)}, u32[]{:S(2)}, u32[]{:S(2)}) collective-permute-start(f32[2,2,256,256]{3,2,1,0:T(8,128)} %pad_maximum_fusion.7), channel_id=1, source_target_pairs={{0,4},{4,8},{8,12},{12,16},{16,20},{20,24},{24,28},{28,32},{32,36}... | collective-permute-start | bytes 3145736 | tf_op jit(solution)/shard_map/while/body/eval_jaxpr/ppermute | solution.py:26
  801.0 11.4 collective-permute-start.2
  802.3 10.5 collective-permute-start.3
  813.4 130.9 %copy-start.11 = (f32[2,4,256,256]{3,2,1,0:T(8,128)S(1)}, f32[2,4,256,256]{3,2,1,0:T(8,128)}, u32[]{:S(2)}) copy-start(f32[2,4,256,256]{3,2,1,0:T(8,128)} %copy-done.10) | copy-start | bytes 6291460 | tf_op jit(solution)/shard_map/while
  956.7 40.2 %copy-start.17 = (f32[8,256]{1,0:T(8,128)}, f32[8,256]{1,0:T(8,128)S(1)}, u32[]{:S(2)}) copy-start(f32[8,256]{1,0:T(8,128)S(1)} %get-tuple-element.736) | copy-start | bytes 24580 | tf_op jit(solution)/shard_map/while
  956.8 40.2 %copy-start.20 = (f32[8,256]{1,0:T(8,128)}, f32[8,256]{1,0:T(8,128)S(1)}, u32[]{:S(2)}) copy-start(f32[8,256]{1,0:T(8,128)S(1)} %get-tuple-element.737) | copy-start | bytes 24580 | tf_op jit(solution)/shard_map/while
  959.1 16.1 %collective-permute-start = (f32[2,2,256,256]{3,2,1,0:T(8,128)S(1)}, f32[2,2,256,256]{3,2,1,0:T(8,128)S(1)}, u32[]{:S(2)}, u32[]{:S(2)}) collective-permute-start(f32[2,2,256,256]{3,2,1,0:T(8,128)S(1)} %pad_maximum_fusion.6), channel_id=1, source_target_pairs={{4,0},{8,4},{12,8},{16,12},{20,16},{24,20},{28,24},{32,28},{36,32}... | collective-permute-start | bytes 3145736 | tf_op jit(solution)/shard_map/while/body/eval_jaxpr/ppermute | solution.py:26
  961.4 13.8 %copy-start.12 = (f32[2,4,256,256]{3,2,1,0:T(8,128)S(1)}, f32[2,4,256,256]{3,2,1,0:T(8,128)}, u32[]{:S(2)}) copy-start(f32[2,4,256,256]{3,2,1,0:T(8,128)} %get-tuple-element.710) | copy-start | bytes 6291460 | tf_op jit(solution)/shard_map/while
  961.4 13.8 %slice-start = ((f32[2,4,256,256]{3,2,1,0:T(8,128)}), f32[2,3,256,256]{3,2,1,0:T(8,128)S(1)}, s32[]{:S(2)}) async-start(f32[2,4,256,256]{3,2,1,0:T(8,128)} %copy-done.15), calls=%async_computation.1 | async-start | bytes 3145728 | tf_op jit(solution)/shard_map/while/body/eval_jaxpr/slice | solution.py:35
  962.1 13.2 copy-start.9
  979.8 148.9 %collective-permute-start.1 = (f32[2,2,256,256]{3,2,1,0:T(8,128)}, f32[2,2,256,256]{3,2,1,0:T(8,128)}, u32[]{:S(2)}, u32[]{:S(2)}) collective-permute-start(f32[2,2,256,256]{3,2,1,0:T(8,128)} %pad_maximum_fusion.7), channel_id=1, source_target_pairs={{0,4},{4,8},{8,12},{12,16},{16,20},{20,24},{24,28},{28,32},{32,36}... | collective-permute-start | bytes 3145736 | tf_op jit(solution)/shard_map/while/body/eval_jaxpr/ppermute | solution.py:26
  984.9 11.6 collective-permute-start.2
  986.2 10.8 collective-permute-start.3
  997.6 130.5 %copy-start.11 = (f32[2,4,256,256]{3,2,1,0:T(8,128)S(1)}, f32[2,4,256,256]{3,2,1,0:T(8,128)}, u32[]{:S(2)}) copy-start(f32[2,4,256,256]{3,2,1,0:T(8,128)} %copy-done.10) | copy-start | bytes 6291460 | tf_op jit(solution)/shard_map/while
  (99 other events, 400.5 us)
Sparse Core Ops, SparseCore 0:
  1140.7 222.4 all-reduce.12
where the time goes:
time: 1370 us
  blocking collectives  778 us (57%)
  waiting for transfers between devices  374 us (27%)
  other arithmetic  95.8 us (7%)
  local copies, waits for them, and re-layouts  53.6 us (4%)
  starting transfers between devices  52.5 us (4%)
  between operations  14.8 us (1%)
    all_gather x6, blocking collectives, port_step(): lax.all_gather(modal_next, 'slab', axis=0, tiled=True)  394 us
    all_gather x6, blocking collectives, port_step(): lax.all_gather(modal_next - modal_now, 'slab', axis=0, tiled=True)  384 us
    psum x1, waiting for transfers between devices, local(): gradient = lax.psum(carried[4], 'run')  220 us
    ppermute x12, waiting for transfers between devices, passed_along(): return lax.ppermute(block, axis, route)  87.8 us
    ppermute x6, waiting for transfers between devices, padded_2(): before = lax.ppermute(last, axis, up)  60.7 us
    ppermute x12, starting transfers between devices, passed_along(): return lax.ppermute(block, axis, route)  36.6 us
    add x6, other arithmetic, update_electric(): electric_z + coefficient * (behind(magnetic_y, 1, lower_y) - behind(magne...  31.7 us
  transfers between devices with their start and end apart: 25, of which 19 were waited for; matrix products, arithmetic and copies ran while one was open for 2% of the time, Pallas kernels for 0%

commit v1 on v0

--- a/solution.py
+++ b/solution.py
@@ -113,7 +113,10 @@
         padded = padded_2(modal_now, (("slab", 0),), 1)
         modal_next = modal_advance(modal_now, modal_old, padded, port_coefficient, profile, forcing)
         incident_e, incident_h = (
-            lax.all_gather(modal_next, "slab", axis=0, tiled=True),
+            jnp.concatenate(
+                lax.all_to_all(jnp.stack([modal_next] * lax.axis_size("slab")), "slab", 0, 0),
+                axis=0,
+            ),
             lax.all_gather(modal_next - modal_now, "slab", axis=0, tiled=True),
         )
         return (modal_next, incident_e, incident_h)

time: 1370 us -> 995 us (0.73)
  blocking collectives: 778 us -> 445 us
  waiting for transfers between devices: 374 us -> 301 us
  starting transfers between devices: 52.5 us -> 71.6 us
    all_gather x6 -> x0, blocking collectives: 394 us -> none  [port_step(): lax.all_gather(modal_next, 'slab', axis=0, tiled=True)]
    psum x1, waiting for transfers between devices: 220 us -> 140 us  [local(): gradient = lax.psum(carried[4], 'run')]
    all_gather x6, blocking collectives: 384 us -> 445 us  [port_step(): lax.all_gather(modal_next - modal_now, 'slab', axis=0, tiled=True)]
    all_to_all x0 -> x6, starting transfers between devices: none -> 30.9 us  [port_step(): lax.all_to_all(jnp.stack([modal_next] * lax.axis_size('slab')), 'slab', 0...]
  transfers between devices with their start and end apart: 25 -> 31, of which waited for: 19 -> 19; matrix products, arithmetic and copies ran while one was open for 2% -> 3% of each run, Pallas kernels for 0% -> 0%
where the time goes in v1:
time: 995 us; the launch traced here: 993 us
  blocking collectives  445 us (45%)
  waiting for transfers between devices  301 us (30%)
  other arithmetic  96.6 us (10%)
  starting transfers between devices  71.6 us (7%)
  local copies, waits for them, and re-layouts  61.1 us (6%)
  between operations  14.8 us (1%)
    all_gather x6, blocking collectives, port_step(): lax.all_gather(modal_next - modal_now, 'slab', axis=0, tiled=True)  445 us
    psum x1, waiting for transfers between devices, local(): gradient = lax.psum(carried[4], 'run')  140 us
    ppermute x12, waiting for transfers between devices, passed_along(): return lax.ppermute(block, axis, route)  87.7 us
    ppermute x6, waiting for transfers between devices, padded_2(): before = lax.ppermute(last, axis, up)  59.7 us
    add x6, other arithmetic, update_electric(): electric_z + coefficient * (behind(magnetic_y, 1, lower_y) - behind(magne...  31.7 us
    all_to_all x6, starting transfers between devices, port_step(): lax.all_to_all(jnp.stack([modal_next] * lax.axis_size('slab')), 'slab', 0...  30.9 us
    ppermute x12, starting transfers between devices, passed_along(): return lax.ppermute(block, axis, route)  24.9 us
    add x6, other arithmetic, advance(): gradient_sum + (electric[0][0] * electric[0][1] + electric[1][0] * electr...  19.9 us
  transfers between devices with their start and end apart: 31, of which 19 were waited for; matrix products, arithmetic and copies ran while one was open for 3% of the time, Pallas kernels for 0%

profile of v1, /device:TPU:1, one launch (start us, length us, event | category | flops | bytes accessed | tf_op | source)
XLA Modules:
  0.0 993.4 jit_solution(13162309904667280901)
XLA Ops:
  7.3 3.4 fusion.32
  14.8 826.8 %while.35 = (s32[]{:T(128)}, f32[2,4,256,256]{3,2,1,0:T(8,128)S(1)}, f32[2,4,256,256]{3,2,1,0:T(8,128)}, f32[2,4,256,256]{3,2,1,0:T(8,128)}, f32[2,4,256,256]{3,...) while((s32[]{:T(128)}, ...), condition=%wide.region_3.0_spmd.clone.clone, body=%wide.region_2.0_spmd.clone.clone.sunk | while | flops 25982984 | bytes 270941312 | solution.py:158
  15.1 2.1 copy-done
  20.4 23.2 %collective-permute-done = f32[2,2,256,256]{3,2,1,0:T(8,128)S(1)} collective-permute-done((f32[2,2,256,256]{3,2,1,0:T(8,128)S(1)}, f32[2,2,256,256]{3,2,1,0:T(8,128)S(1)}, u32[]{:S(2)}, u32[]{:S(2)}) %collective-permute-start) | collective-permute-done | bytes 1048608 | tf_op jit(solution)/shard_map/while/body/eval_jaxpr/ppermute | solution.py:26
  43.7 2.2 select_subtract_fusion.2
  48.2 5.4 collective-permute-start.1
  56.7 17.1 %collective-permute-done.2 = f32[1,256]{1,0:T(1,128)S(1)} collective-permute-done((f32[1,256]{1,0:T(1,128)S(1)}, f32[1,256]{1,0:T(1,128)S(1)}, u32[]{:S(2)}, u32[]{:S(2)}) %collective-permute-start.2) | collective-permute-done | bytes 1056 | tf_op jit(solution)/shard_map/while/body/eval_jaxpr/ppermute | solution.py:17
  75.7 11.5 %all-to-all-start = ((f32[32,8,256]{2,1,0:T(8,128)}), f32[32,8,256]{2,1,0:T(8,128)S(1)}, u32[]{:S(2)}, u32[]{:S(2)}) async-start(f32[32,8,256]{2,1,0:T(8,128)} %stack.9), calls=%async_computation | async-start | bytes 524288 | tf_op jit(solution)/shard_map/while/body/eval_jaxpr/all_to_all | solution.py:117
  87.9 73.8 %all_gather.13 = f32[256,256]{1,0:T(8,128)} all-gather(f32[8,256]{1,0:T(8,128)S(1)} %get-tuple-element.676), channel_id=1, replica_groups=mesh['slab'=32,'run'=4] {'slab'}, dimensions={0}, use_global_device_ids=true | all-gather | bytes 270336 | tf_op jit(solution)/shard_map/while/body/eval_jaxpr/all_gather | solution.py:120
  164.8 2.5 fusion.40
  167.3 5.3 fusion.43
  175.0 2.0 broadcast_select_fusion.4
  180.5 12.4 %collective-permute-done = f32[2,2,256,256]{3,2,1,0:T(8,128)S(1)} collective-permute-done((f32[2,2,256,256]{3,2,1,0:T(8,128)S(1)}, f32[2,2,256,256]{3,2,1,0:T(8,128)S(1)}, u32[]{:S(2)}, u32[]{:S(2)}) %collective-permute-start) | collective-permute-done | bytes 1048608 | tf_op jit(solution)/shard_map/while/body/eval_jaxpr/ppermute | solution.py:26
  193.0 2.2 select_subtract_fusion.2
  197.5 2.4 collective-permute-start.1
  202.7 8.3 collective-permute-done.2
  211.0 11.1 %collective-permute-done.3 = f32[1,256]{1,0:T(1,128)S(1)} collective-permute-done((f32[1,256]{1,0:T(1,128)S(1)}, f32[1,256]{1,0:T(1,128)S(1)}, u32[]{:S(2)}, u32[]{:S(2)}) %collective-permute-start.3) | collective-permute-done | bytes 1056 | tf_op jit(solution)/shard_map/while/body/eval_jaxpr/ppermute | solution.py:18
  222.9 3.9 all-to-all-start
  227.4 74.3 %all_gather.13 = f32[256,256]{1,0:T(8,128)} all-gather(f32[8,256]{1,0:T(8,128)S(1)} %get-tuple-element.676), channel_id=1, replica_groups=mesh['slab'=32,'run'=4] {'slab'}, dimensions={0}, use_global_device_ids=true | all-gather | bytes 270336 | tf_op jit(solution)/shard_map/while/body/eval_jaxpr/all_gather | solution.py:120
  304.8 2.5 fusion.40
  307.3 5.3 fusion.43
  312.6 3.6 fusion.44
  316.3 2.0 broadcast_select_fusion.4
  321.8 13.0 %collective-permute-done = f32[2,2,256,256]{3,2,1,0:T(8,128)S(1)} collective-permute-done((f32[2,2,256,256]{3,2,1,0:T(8,128)S(1)}, f32[2,2,256,256]{3,2,1,0:T(8,128)S(1)}, u32[]{:S(2)}, u32[]{:S(2)}) %collective-permute-start) | collective-permute-done | bytes 1048608 | tf_op jit(solution)/shard_map/while/body/eval_jaxpr/ppermute | solution.py:26
  335.0 2.2 select_subtract_fusion.2
  339.5 2.3 collective-permute-start.1
  344.5 8.3 collective-permute-done.2
  353.8 3.9 all-to-all-start
  358.2 74.4 %all_gather.13 = f32[256,256]{1,0:T(8,128)} all-gather(f32[8,256]{1,0:T(8,128)S(1)} %get-tuple-element.676), channel_id=1, replica_groups=mesh['slab'=32,'run'=4] {'slab'}, dimensions={0}, use_global_device_ids=true | all-gather | bytes 270336 | tf_op jit(solution)/shard_map/while/body/eval_jaxpr/all_gather | solution.py:120
  435.8 2.5 fusion.40
  438.4 5.3 fusion.43
  443.7 3.6 fusion.44
  447.4 2.0 broadcast_select_fusion.4
  452.9 13.1 %collective-permute-done = f32[2,2,256,256]{3,2,1,0:T(8,128)S(1)} collective-permute-done((f32[2,2,256,256]{3,2,1,0:T(8,128)S(1)}, f32[2,2,256,256]{3,2,1,0:T(8,128)S(1)}, u32[]{:S(2)}, u32[]{:S(2)}) %collective-permute-start) | collective-permute-done | bytes 1048608 | tf_op jit(solution)/shard_map/while/body/eval_jaxpr/ppermute | solution.py:26
  466.1 2.2 select_subtract_fusion.2
  470.7 2.3 collective-permute-start.1
  475.7 8.6 collective-permute-done.2
  485.6 3.9 all-to-all-start
  490.1 74.3 %all_gather.13 = f32[256,256]{1,0:T(8,128)} all-gather(f32[8,256]{1,0:T(8,128)S(1)} %get-tuple-element.676), channel_id=1, replica_groups=mesh['slab'=32,'run'=4] {'slab'}, dimensions={0}, use_global_device_ids=true | all-gather | bytes 270336 | tf_op jit(solution)/shard_map/while/body/eval_jaxpr/all_gather | solution.py:120
  567.5 2.5 fusion.40
  570.1 5.3 fusion.43
  575.4 3.6 fusion.44
  579.1 2.0 broadcast_select_fusion.4
  584.6 12.7 %collective-permute-done = f32[2,2,256,256]{3,2,1,0:T(8,128)S(1)} collective-permute-done((f32[2,2,256,256]{3,2,1,0:T(8,128)S(1)}, f32[2,2,256,256]{3,2,1,0:T(8,128)S(1)}, u32[]{:S(2)}, u32[]{:S(2)}) %collective-permute-start) | collective-permute-done | bytes 1048608 | tf_op jit(solution)/shard_map/while/body/eval_jaxpr/ppermute | solution.py:26
  597.5 2.2 select_subtract_fusion.2
  602.0 2.4 collective-permute-start.1
  607.2 8.7 collective-permute-done.2
  617.0 3.9 all-to-all-start
  621.5 74.2 %all_gather.13 = f32[256,256]{1,0:T(8,128)} all-gather(f32[8,256]{1,0:T(8,128)S(1)} %get-tuple-element.676), channel_id=1, replica_groups=mesh['slab'=32,'run'=4] {'slab'}, dimensions={0}, use_global_device_ids=true | all-gather | bytes 270336 | tf_op jit(solution)/shard_map/while/body/eval_jaxpr/all_gather | solution.py:120
  698.9 2.5 fusion.40
  701.4 5.3 fusion.43
  706.7 3.6 fusion.44
  715.9 13.3 %collective-permute-done = f32[2,2,256,256]{3,2,1,0:T(8,128)S(1)} collective-permute-done((f32[2,2,256,256]{3,2,1,0:T(8,128)S(1)}, f32[2,2,256,256]{3,2,1,0:T(8,128)S(1)}, u32[]{:S(2)}, u32[]{:S(2)}) %collective-permute-start) | collective-permute-done | bytes 1048608 | tf_op jit(solution)/shard_map/while/body/eval_jaxpr/ppermute | solution.py:26
  729.4 2.2 select_subtract_fusion.2
  733.9 2.3 collective-permute-start.1
  738.9 8.7 collective-permute-done.2
  748.5 3.9 all-to-all-start
  753.0 73.9 %all_gather.13 = f32[256,256]{1,0:T(8,128)} all-gather(f32[8,256]{1,0:T(8,128)S(1)} %get-tuple-element.676), channel_id=1, replica_groups=mesh['slab'=32,'run'=4] {'slab'}, dimensions={0}, use_global_device_ids=true | all-gather | bytes 270336 | tf_op jit(solution)/shard_map/while/body/eval_jaxpr/all_gather | solution.py:120
  830.0 2.5 fusion.40
  832.6 5.3 fusion.43
  837.9 3.6 fusion.44
  841.6 2.3 slice.373
  843.9 140.4 %all-reduce.13.cloned.1.call-done = f32[4,256,256]{2,1,0:T(8,128)} async-done(((f32[4,256,256]{2,1,0:T(8,128)}), f32[4,256,256]{2,1,0:T(8,128)}) %all-reduce.13.cloned.1.call-update) | async-done | bytes 1048592 | tf_op jit(solution)/shard_map/psum | solution.py:164
  984.3 2.3 copy.42
  (460 shorter events, 88.0 us)
Async XLA Ops:
  7.2 977.1 %all-reduce.13.cloned.1.call-start = ((), (), s32[]{:S(2)}) async-start(), calls=%async_computation.1 | async-start | bytes 2097152 | tf_op jit(solution)/shard_map/psum | solution.py:164
  14.8 60.2 %copy-start.18 = (f32[8,256]{1,0:T(8,128)}, f32[8,256]{1,0:T(8,128)S(1)}, u32[]{:S(2)}) copy-start(f32[8,256]{1,0:T(8,128)S(1)} %get-tuple-element.736) | copy-start | bytes 24580 | tf_op jit(solution)/shard_map/while
  14.8 60.2 %copy-start.21 = (f32[8,256]{1,0:T(8,128)}, f32[8,256]{1,0:T(8,128)S(1)}, u32[]{:S(2)}) copy-start(f32[8,256]{1,0:T(8,128)S(1)} %get-tuple-element.737) | copy-start | bytes 24580 | tf_op jit(solution)/shard_map/while
  17.2 26.3 %collective-permute-start = (f32[2,2,256,256]{3,2,1,0:T(8,128)S(1)}, f32[2,2,256,256]{3,2,1,0:T(8,128)S(1)}, u32[]{:S(2)}, u32[]{:S(2)}) collective-permute-start(f32[2,2,256,256]{3,2,1,0:T(8,128)S(1)} %pad_maximum_fusion.6), channel_id=1, source_target_pairs={{4,0},{8,4},{12,8},{16,12},{20,16},{24,20},{28,24},{32,28},{36,32}... | collective-permute-start | bytes 3145736 | tf_op jit(solution)/shard_map/while/body/eval_jaxpr/ppermute | solution.py:26
  19.6 24.1 %copy-start.12 = (f32[2,4,256,256]{3,2,1,0:T(8,128)S(1)}, f32[2,4,256,256]{3,2,1,0:T(8,128)}, u32[]{:S(2)}) copy-start(f32[2,4,256,256]{3,2,1,0:T(8,128)} %get-tuple-element.710) | copy-start | bytes 6291460 | tf_op jit(solution)/shard_map/while
  19.6 24.1 %slice-start = ((f32[2,4,256,256]{3,2,1,0:T(8,128)}), f32[2,3,256,256]{3,2,1,0:T(8,128)S(1)}, s32[]{:S(2)}) async-start(f32[2,4,256,256]{3,2,1,0:T(8,128)} %copy-done.15), calls=%async_computation.2 | async-start | bytes 3145728 | tf_op jit(solution)/shard_map/while/body/eval_jaxpr/slice | solution.py:35
  20.2 23.5 %copy-start.6 = (f32[2,4,256,256]{3,2,1,0:T(8,128)S(1)}, f32[2,4,256,256]{3,2,1,0:T(8,128)}, u32[]{:S(2)}) copy-start(f32[2,4,256,256]{3,2,1,0:T(8,128)} %get-tuple-element.708) | copy-start | bytes 6291460 | tf_op jit(solution)/shard_map/while
  20.2 23.5 %copy-start.9 = (f32[2,4,256,256]{3,2,1,0:T(8,128)S(1)}, f32[2,4,256,256]{3,2,1,0:T(8,128)}, u32[]{:S(2)}) copy-start(f32[2,4,256,256]{3,2,1,0:T(8,128)} %get-tuple-element.709) | copy-start | bytes 6291460 | tf_op jit(solution)/shard_map/while
  20.4 23.3 %copy-start.3 = (f32[2,4,256,256]{3,2,1,0:T(8,128)S(1)}, f32[2,4,256,256]{3,2,1,0:T(8,128)}, u32[]{:S(2)}) copy-start(f32[2,4,256,256]{3,2,1,0:T(8,128)} %get-tuple-element.706) | copy-start | bytes 6291460 | tf_op jit(solution)/shard_map/while
  48.2 116.6 %collective-permute-start.1 = (f32[2,2,256,256]{3,2,1,0:T(8,128)}, f32[2,2,256,256]{3,2,1,0:T(8,128)}, u32[]{:S(2)}, u32[]{:S(2)}) collective-permute-start(f32[2,2,256,256]{3,2,1,0:T(8,128)} %pad_maximum_fusion.7), channel_id=1, source_target_pairs={{0,4},{4,8},{8,12},{12,16},{16,20},{20,24},{24,28},{28,32},{32,36}... | collective-permute-start | bytes 3145736 | tf_op jit(solution)/shard_map/while/body/eval_jaxpr/ppermute | solution.py:26
  53.6 20.2 %collective-permute-start.2 = (f32[1,256]{1,0:T(1,128)S(1)}, f32[1,256]{1,0:T(1,128)S(1)}, u32[]{:S(2)}, u32[]{:S(2)}) collective-permute-start(f32[1,256]{1,0:T(1,128)S(1)} %get-tuple-element.673), channel_id=1, source_target_pairs={{0,4},{4,8},{8,12},{12,16},{16,20},{20,24},{24,28},{28,32},{32,36}... | collective-permute-start | bytes 3080 | tf_op jit(solution)/shard_map/while/body/eval_jaxpr/ppermute | solution.py:17
  55.3 19.6 %collective-permute-start.3 = (f32[1,256]{1,0:T(1,128)S(1)}, f32[1,256]{1,0:T(1,128)S(1)}, u32[]{:S(2)}, u32[]{:S(2)}) collective-permute-start(f32[1,256]{1,0:T(1,128)S(1)} %get-tuple-element.674), channel_id=1, source_target_pairs={{4,0},{8,4},{12,8},{16,12},{20,16},{24,20},{28,24},{32,28},{36,32}... | collective-permute-start | bytes 3080 | tf_op jit(solution)/shard_map/while/body/eval_jaxpr/ppermute | solution.py:18
  75.7 85.9 %all-to-all-start = ((f32[32,8,256]{2,1,0:T(8,128)}), f32[32,8,256]{2,1,0:T(8,128)S(1)}, u32[]{:S(2)}, u32[]{:S(2)}) async-start(f32[32,8,256]{2,1,0:T(8,128)} %stack.9), calls=%async_computation | async-start | bytes 524288 | tf_op jit(solution)/shard_map/while/body/eval_jaxpr/all_to_all | solution.py:117
  175.0 47.1 %copy-start.18 = (f32[8,256]{1,0:T(8,128)}, f32[8,256]{1,0:T(8,128)S(1)}, u32[]{:S(2)}) copy-start(f32[8,256]{1,0:T(8,128)S(1)} %get-tuple-element.736) | copy-start | bytes 24580 | tf_op jit(solution)/shard_map/while
  175.0 47.1 %copy-start.21 = (f32[8,256]{1,0:T(8,128)}, f32[8,256]{1,0:T(8,128)S(1)}, u32[]{:S(2)}) copy-start(f32[8,256]{1,0:T(8,128)S(1)} %get-tuple-element.737) | copy-start | bytes 24580 | tf_op jit(solution)/shard_map/while
  177.3 15.5 %collective-permute-start = (f32[2,2,256,256]{3,2,1,0:T(8,128)S(1)}, f32[2,2,256,256]{3,2,1,0:T(8,128)S(1)}, u32[]{:S(2)}, u32[]{:S(2)}) collective-permute-start(f32[2,2,256,256]{3,2,1,0:T(8,128)S(1)} %pad_maximum_fusion.6), channel_id=1, source_target_pairs={{4,0},{8,4},{12,8},{16,12},{20,16},{24,20},{28,24},{32,28},{36,32}... | collective-permute-start | bytes 3145736 | tf_op jit(solution)/shard_map/while/body/eval_jaxpr/ppermute | solution.py:26
  179.7 13.3 %copy-start.12 = (f32[2,4,256,256]{3,2,1,0:T(8,128)S(1)}, f32[2,4,256,256]{3,2,1,0:T(8,128)}, u32[]{:S(2)}) copy-start(f32[2,4,256,256]{3,2,1,0:T(8,128)} %get-tuple-element.710) | copy-start | bytes 6291460 | tf_op jit(solution)/shard_map/while
  197.5 107.2 %collective-permute-start.1 = (f32[2,2,256,256]{3,2,1,0:T(8,128)}, f32[2,2,256,256]{3,2,1,0:T(8,128)}, u32[]{:S(2)}, u32[]{:S(2)}) collective-permute-start(f32[2,2,256,256]{3,2,1,0:T(8,128)} %pad_maximum_fusion.7), channel_id=1, source_target_pairs={{0,4},{4,8},{8,12},{12,16},{16,20},{20,24},{24,28},{28,32},{32,36}... | collective-permute-start | bytes 3145736 | tf_op jit(solution)/shard_map/while/body/eval_jaxpr/ppermute | solution.py:26
  200.0 11.0 %collective-permute-start.2 = (f32[1,256]{1,0:T(1,128)S(1)}, f32[1,256]{1,0:T(1,128)S(1)}, u32[]{:S(2)}, u32[]{:S(2)}) collective-permute-start(f32[1,256]{1,0:T(1,128)S(1)} %get-tuple-element.673), channel_id=1, source_target_pairs={{0,4},{4,8},{8,12},{12,16},{16,20},{20,24},{24,28},{28,32},{32,36}... | collective-permute-start | bytes 3080 | tf_op jit(solution)/shard_map/while/body/eval_jaxpr/ppermute | solution.py:17
  201.3 20.8 %collective-permute-start.3 = (f32[1,256]{1,0:T(1,128)S(1)}, f32[1,256]{1,0:T(1,128)S(1)}, u32[]{:S(2)}, u32[]{:S(2)}) collective-permute-start(f32[1,256]{1,0:T(1,128)S(1)} %get-tuple-element.674), channel_id=1, source_target_pairs={{4,0},{8,4},{12,8},{16,12},{20,16},{24,20},{28,24},{32,28},{36,32}... | collective-permute-start | bytes 3080 | tf_op jit(solution)/shard_map/while/body/eval_jaxpr/ppermute | solution.py:18
  222.9 78.7 %all-to-all-start = ((f32[32,8,256]{2,1,0:T(8,128)}), f32[32,8,256]{2,1,0:T(8,128)S(1)}, u32[]{:S(2)}, u32[]{:S(2)}) async-start(f32[32,8,256]{2,1,0:T(8,128)} %stack.9), calls=%async_computation | async-start | bytes 524288 | tf_op jit(solution)/shard_map/while/body/eval_jaxpr/all_to_all | solution.py:117
  316.3 36.7 %copy-start.18 = (f32[8,256]{1,0:T(8,128)}, f32[8,256]{1,0:T(8,128)S(1)}, u32[]{:S(2)}) copy-start(f32[8,256]{1,0:T(8,128)S(1)} %get-tuple-element.736) | copy-start | bytes 24580 | tf_op jit(solution)/shard_map/while
  316.3 36.7 %copy-start.21 = (f32[8,256]{1,0:T(8,128)}, f32[8,256]{1,0:T(8,128)S(1)}, u32[]{:S(2)}) copy-start(f32[8,256]{1,0:T(8,128)S(1)} %get-tuple-element.737) | copy-start | bytes 24580 | tf_op jit(solution)/shard_map/while
  318.7 16.2 %collective-permute-start = (f32[2,2,256,256]{3,2,1,0:T(8,128)S(1)}, f32[2,2,256,256]{3,2,1,0:T(8,128)S(1)}, u32[]{:S(2)}, u32[]{:S(2)}) collective-permute-start(f32[2,2,256,256]{3,2,1,0:T(8,128)S(1)} %pad_maximum_fusion.6), channel_id=1, source_target_pairs={{4,0},{8,4},{12,8},{16,12},{20,16},{24,20},{28,24},{32,28},{36,32}... | collective-permute-start | bytes 3145736 | tf_op jit(solution)/shard_map/while/body/eval_jaxpr/ppermute | solution.py:26
  321.0 14.0 %copy-start.12 = (f32[2,4,256,256]{3,2,1,0:T(8,128)S(1)}, f32[2,4,256,256]{3,2,1,0:T(8,128)}, u32[]{:S(2)}) copy-start(f32[2,4,256,256]{3,2,1,0:T(8,128)} %get-tuple-element.710) | copy-start | bytes 6291460 | tf_op jit(solution)/shard_map/while
  321.0 14.0 %slice-start = ((f32[2,4,256,256]{3,2,1,0:T(8,128)}), f32[2,3,256,256]{3,2,1,0:T(8,128)S(1)}, s32[]{:S(2)}) async-start(f32[2,4,256,256]{3,2,1,0:T(8,128)} %copy-done.15), calls=%async_computation.2 | async-start | bytes 3145728 | tf_op jit(solution)/shard_map/while/body/eval_jaxpr/slice | solution.py:35
  321.6 13.4 %copy-start.6 = (f32[2,4,256,256]{3,2,1,0:T(8,128)S(1)}, f32[2,4,256,256]{3,2,1,0:T(8,128)}, u32[]{:S(2)}) copy-start(f32[2,4,256,256]{3,2,1,0:T(8,128)} %get-tuple-element.708) | copy-start | bytes 6291460 | tf_op jit(solution)/shard_map/while
  321.6 13.4 %copy-start.9 = (f32[2,4,256,256]{3,2,1,0:T(8,128)S(1)}, f32[2,4,256,256]{3,2,1,0:T(8,128)}, u32[]{:S(2)}) copy-start(f32[2,4,256,256]{3,2,1,0:T(8,128)} %get-tuple-element.709) | copy-start | bytes 6291460 | tf_op jit(solution)/shard_map/while
  339.5 96.3 %collective-permute-start.1 = (f32[2,2,256,256]{3,2,1,0:T(8,128)}, f32[2,2,256,256]{3,2,1,0:T(8,128)}, u32[]{:S(2)}, u32[]{:S(2)}) collective-permute-start(f32[2,2,256,256]{3,2,1,0:T(8,128)} %pad_maximum_fusion.7), channel_id=1, source_target_pairs={{0,4},{4,8},{8,12},{12,16},{16,20},{20,24},{24,28},{28,32},{32,36}... | collective-permute-start | bytes 3145736 | tf_op jit(solution)/shard_map/while/body/eval_jaxpr/ppermute | solution.py:26
  341.8 11.0 %collective-permute-start.2 = (f32[1,256]{1,0:T(1,128)S(1)}, f32[1,256]{1,0:T(1,128)S(1)}, u32[]{:S(2)}, u32[]{:S(2)}) collective-permute-start(f32[1,256]{1,0:T(1,128)S(1)} %get-tuple-element.673), channel_id=1, source_target_pairs={{0,4},{4,8},{8,12},{12,16},{16,20},{20,24},{24,28},{28,32},{32,36}... | collective-permute-start | bytes 3080 | tf_op jit(solution)/shard_map/while/body/eval_jaxpr/ppermute | solution.py:17
  343.1 9.9 collective-permute-start.3
  353.8 78.9 %all-to-all-start = ((f32[32,8,256]{2,1,0:T(8,128)}), f32[32,8,256]{2,1,0:T(8,128)S(1)}, u32[]{:S(2)}, u32[]{:S(2)}) async-start(f32[32,8,256]{2,1,0:T(8,128)} %stack.9), calls=%async_computation | async-start | bytes 524288 | tf_op jit(solution)/shard_map/while/body/eval_jaxpr/all_to_all | solution.py:117
  447.4 37.4 %copy-start.18 = (f32[8,256]{1,0:T(8,128)}, f32[8,256]{1,0:T(8,128)S(1)}, u32[]{:S(2)}) copy-start(f32[8,256]{1,0:T(8,128)S(1)} %get-tuple-element.736) | copy-start | bytes 24580 | tf_op jit(solution)/shard_map/while
  447.4 37.4 %copy-start.21 = (f32[8,256]{1,0:T(8,128)}, f32[8,256]{1,0:T(8,128)S(1)}, u32[]{:S(2)}) copy-start(f32[8,256]{1,0:T(8,128)S(1)} %get-tuple-element.737) | copy-start | bytes 24580 | tf_op jit(solution)/shard_map/while
  449.7 16.3 %collective-permute-start = (f32[2,2,256,256]{3,2,1,0:T(8,128)S(1)}, f32[2,2,256,256]{3,2,1,0:T(8,128)S(1)}, u32[]{:S(2)}, u32[]{:S(2)}) collective-permute-start(f32[2,2,256,256]{3,2,1,0:T(8,128)S(1)} %pad_maximum_fusion.6), channel_id=1, source_target_pairs={{4,0},{8,4},{12,8},{16,12},{20,16},{24,20},{28,24},{32,28},{36,32}... | collective-permute-start | bytes 3145736 | tf_op jit(solution)/shard_map/while/body/eval_jaxpr/ppermute | solution.py:26
  452.0 14.1 %copy-start.12 = (f32[2,4,256,256]{3,2,1,0:T(8,128)S(1)}, f32[2,4,256,256]{3,2,1,0:T(8,128)}, u32[]{:S(2)}) copy-start(f32[2,4,256,256]{3,2,1,0:T(8,128)} %get-tuple-element.710) | copy-start | bytes 6291460 | tf_op jit(solution)/shard_map/while
  452.1 14.1 %slice-start = ((f32[2,4,256,256]{3,2,1,0:T(8,128)}), f32[2,3,256,256]{3,2,1,0:T(8,128)S(1)}, s32[]{:S(2)}) async-start(f32[2,4,256,256]{3,2,1,0:T(8,128)} %copy-done.15), calls=%async_computation.2 | async-start | bytes 3145728 | tf_op jit(solution)/shard_map/while/body/eval_jaxpr/slice | solution.py:35
  452.7 13.5 %copy-start.6 = (f32[2,4,256,256]{3,2,1,0:T(8,128)S(1)}, f32[2,4,256,256]{3,2,1,0:T(8,128)}, u32[]{:S(2)}) copy-start(f32[2,4,256,256]{3,2,1,0:T(8,128)} %get-tuple-element.708) | copy-start | bytes 6291460 | tf_op jit(solution)/shard_map/while
  452.7 13.5 %copy-start.9 = (f32[2,4,256,256]{3,2,1,0:T(8,128)S(1)}, f32[2,4,256,256]{3,2,1,0:T(8,128)}, u32[]{:S(2)}) copy-start(f32[2,4,256,256]{3,2,1,0:T(8,128)} %get-tuple-element.709) | copy-start | bytes 6291460 | tf_op jit(solution)/shard_map/while
  470.7 96.9 %collective-permute-start.1 = (f32[2,2,256,256]{3,2,1,0:T(8,128)}, f32[2,2,256,256]{3,2,1,0:T(8,128)}, u32[]{:S(2)}, u32[]{:S(2)}) collective-permute-start(f32[2,2,256,256]{3,2,1,0:T(8,128)} %pad_maximum_fusion.7), channel_id=1, source_target_pairs={{0,4},{4,8},{8,12},{12,16},{16,20},{20,24},{24,28},{28,32},{32,36}... | collective-permute-start | bytes 3145736 | tf_op jit(solution)/shard_map/while/body/eval_jaxpr/ppermute | solution.py:26
  472.9 11.3 %collective-permute-start.2 = (f32[1,256]{1,0:T(1,128)S(1)}, f32[1,256]{1,0:T(1,128)S(1)}, u32[]{:S(2)}, u32[]{:S(2)}) collective-permute-start(f32[1,256]{1,0:T(1,128)S(1)} %get-tuple-element.673), channel_id=1, source_target_pairs={{0,4},{4,8},{8,12},{12,16},{16,20},{20,24},{24,28},{28,32},{32,36}... | collective-permute-start | bytes 3080 | tf_op jit(solution)/shard_map/while/body/eval_jaxpr/ppermute | solution.py:17
  474.2 10.6 %collective-permute-start.3 = (f32[1,256]{1,0:T(1,128)S(1)}, f32[1,256]{1,0:T(1,128)S(1)}, u32[]{:S(2)}, u32[]{:S(2)}) collective-permute-start(f32[1,256]{1,0:T(1,128)S(1)} %get-tuple-element.674), channel_id=1, source_target_pairs={{4,0},{8,4},{12,8},{16,12},{20,16},{24,20},{28,24},{32,28},{36,32}... | collective-permute-start | bytes 3080 | tf_op jit(solution)/shard_map/while/body/eval_jaxpr/ppermute | solution.py:18
  485.6 78.8 %all-to-all-start = ((f32[32,8,256]{2,1,0:T(8,128)}), f32[32,8,256]{2,1,0:T(8,128)S(1)}, u32[]{:S(2)}, u32[]{:S(2)}) async-start(f32[32,8,256]{2,1,0:T(8,128)} %stack.9), calls=%async_computation | async-start | bytes 524288 | tf_op jit(solution)/shard_map/while/body/eval_jaxpr/all_to_all | solution.py:117
  579.1 37.1 %copy-start.18 = (f32[8,256]{1,0:T(8,128)}, f32[8,256]{1,0:T(8,128)S(1)}, u32[]{:S(2)}) copy-start(f32[8,256]{1,0:T(8,128)S(1)} %get-tuple-element.736) | copy-start | bytes 24580 | tf_op jit(solution)/shard_map/while
  579.1 37.1 %copy-start.21 = (f32[8,256]{1,0:T(8,128)}, f32[8,256]{1,0:T(8,128)S(1)}, u32[]{:S(2)}) copy-start(f32[8,256]{1,0:T(8,128)S(1)} %get-tuple-element.737) | copy-start | bytes 24580 | tf_op jit(solution)/shard_map/while
  581.4 15.9 %collective-permute-start = (f32[2,2,256,256]{3,2,1,0:T(8,128)S(1)}, f32[2,2,256,256]{3,2,1,0:T(8,128)S(1)}, u32[]{:S(2)}, u32[]{:S(2)}) collective-permute-start(f32[2,2,256,256]{3,2,1,0:T(8,128)S(1)} %pad_maximum_fusion.6), channel_id=1, source_target_pairs={{4,0},{8,4},{12,8},{16,12},{20,16},{24,20},{28,24},{32,28},{36,32}... | collective-permute-start | bytes 3145736 | tf_op jit(solution)/shard_map/while/body/eval_jaxpr/ppermute | solution.py:26
  583.8 13.7 %copy-start.12 = (f32[2,4,256,256]{3,2,1,0:T(8,128)S(1)}, f32[2,4,256,256]{3,2,1,0:T(8,128)}, u32[]{:S(2)}) copy-start(f32[2,4,256,256]{3,2,1,0:T(8,128)} %get-tuple-element.710) | copy-start | bytes 6291460 | tf_op jit(solution)/shard_map/while
  583.8 13.7 %slice-start = ((f32[2,4,256,256]{3,2,1,0:T(8,128)}), f32[2,3,256,256]{3,2,1,0:T(8,128)S(1)}, s32[]{:S(2)}) async-start(f32[2,4,256,256]{3,2,1,0:T(8,128)} %copy-done.15), calls=%async_computation.2 | async-start | bytes 3145728 | tf_op jit(solution)/shard_map/while/body/eval_jaxpr/slice | solution.py:35
  602.0 96.9 %collective-permute-start.1 = (f32[2,2,256,256]{3,2,1,0:T(8,128)}, f32[2,2,256,256]{3,2,1,0:T(8,128)}, u32[]{:S(2)}, u32[]{:S(2)}) collective-permute-start(f32[2,2,256,256]{3,2,1,0:T(8,128)} %pad_maximum_fusion.7), channel_id=1, source_target_pairs={{0,4},{4,8},{8,12},{12,16},{16,20},{20,24},{24,28},{28,32},{32,36}... | collective-permute-start | bytes 3145736 | tf_op jit(solution)/shard_map/while/body/eval_jaxpr/ppermute | solution.py:26
  604.4 11.4 %collective-permute-start.2 = (f32[1,256]{1,0:T(1,128)S(1)}, f32[1,256]{1,0:T(1,128)S(1)}, u32[]{:S(2)}, u32[]{:S(2)}) collective-permute-start(f32[1,256]{1,0:T(1,128)S(1)} %get-tuple-element.673), channel_id=1, source_target_pairs={{0,4},{4,8},{8,12},{12,16},{16,20},{20,24},{24,28},{28,32},{32,36}... | collective-permute-start | bytes 3080 | tf_op jit(solution)/shard_map/while/body/eval_jaxpr/ppermute | solution.py:17
  605.7 10.5 %collective-permute-start.3 = (f32[1,256]{1,0:T(1,128)S(1)}, f32[1,256]{1,0:T(1,128)S(1)}, u32[]{:S(2)}, u32[]{:S(2)}) collective-permute-start(f32[1,256]{1,0:T(1,128)S(1)} %get-tuple-element.674), channel_id=1, source_target_pairs={{4,0},{8,4},{12,8},{16,12},{20,16},{24,20},{28,24},{32,28},{36,32}... | collective-permute-start | bytes 3080 | tf_op jit(solution)/shard_map/while/body/eval_jaxpr/ppermute | solution.py:18
  617.0 78.7 %all-to-all-start = ((f32[32,8,256]{2,1,0:T(8,128)}), f32[32,8,256]{2,1,0:T(8,128)S(1)}, u32[]{:S(2)}, u32[]{:S(2)}) async-start(f32[32,8,256]{2,1,0:T(8,128)} %stack.9), calls=%async_computation | async-start | bytes 524288 | tf_op jit(solution)/shard_map/while/body/eval_jaxpr/all_to_all | solution.py:117
  710.4 37.3 %copy-start.18 = (f32[8,256]{1,0:T(8,128)}, f32[8,256]{1,0:T(8,128)S(1)}, u32[]{:S(2)}) copy-start(f32[8,256]{1,0:T(8,128)S(1)} %get-tuple-element.736) | copy-start | bytes 24580 | tf_op jit(solution)/shard_map/while
  710.4 37.3 %copy-start.21 = (f32[8,256]{1,0:T(8,128)}, f32[8,256]{1,0:T(8,128)S(1)}, u32[]{:S(2)}) copy-start(f32[8,256]{1,0:T(8,128)S(1)} %get-tuple-element.737) | copy-start | bytes 24580 | tf_op jit(solution)/shard_map/while
  712.8 16.5 %collective-permute-start = (f32[2,2,256,256]{3,2,1,0:T(8,128)S(1)}, f32[2,2,256,256]{3,2,1,0:T(8,128)S(1)}, u32[]{:S(2)}, u32[]{:S(2)}) collective-permute-start(f32[2,2,256,256]{3,2,1,0:T(8,128)S(1)} %pad_maximum_fusion.6), channel_id=1, source_target_pairs={{4,0},{8,4},{12,8},{16,12},{20,16},{24,20},{28,24},{32,28},{36,32}... | collective-permute-start | bytes 3145736 | tf_op jit(solution)/shard_map/while/body/eval_jaxpr/ppermute | solution.py:26
  715.1 14.2 %copy-start.12 = (f32[2,4,256,256]{3,2,1,0:T(8,128)S(1)}, f32[2,4,256,256]{3,2,1,0:T(8,128)}, u32[]{:S(2)}) copy-start(f32[2,4,256,256]{3,2,1,0:T(8,128)} %get-tuple-element.710) | copy-start | bytes 6291460 | tf_op jit(solution)/shard_map/while
  715.1 14.2 %slice-start = ((f32[2,4,256,256]{3,2,1,0:T(8,128)}), f32[2,3,256,256]{3,2,1,0:T(8,128)S(1)}, s32[]{:S(2)}) async-start(f32[2,4,256,256]{3,2,1,0:T(8,128)} %copy-done.15), calls=%async_computation.2 | async-start | bytes 3145728 | tf_op jit(solution)/shard_map/while/body/eval_jaxpr/slice | solution.py:35
  715.7 13.6 %copy-start.6 = (f32[2,4,256,256]{3,2,1,0:T(8,128)S(1)}, f32[2,4,256,256]{3,2,1,0:T(8,128)}, u32[]{:S(2)}) copy-start(f32[2,4,256,256]{3,2,1,0:T(8,128)} %get-tuple-element.708) | copy-start | bytes 6291460 | tf_op jit(solution)/shard_map/while
  715.7 13.6 %copy-start.9 = (f32[2,4,256,256]{3,2,1,0:T(8,128)S(1)}, f32[2,4,256,256]{3,2,1,0:T(8,128)}, u32[]{:S(2)}) copy-start(f32[2,4,256,256]{3,2,1,0:T(8,128)} %get-tuple-element.709) | copy-start | bytes 6291460 | tf_op jit(solution)/shard_map/while
  715.9 13.4 %copy-start.3 = (f32[2,4,256,256]{3,2,1,0:T(8,128)S(1)}, f32[2,4,256,256]{3,2,1,0:T(8,128)}, u32[]{:S(2)}) copy-start(f32[2,4,256,256]{3,2,1,0:T(8,128)} %get-tuple-element.706) | copy-start | bytes 6291460 | tf_op jit(solution)/shard_map/while
  733.9 96.2 %collective-permute-start.1 = (f32[2,2,256,256]{3,2,1,0:T(8,128)}, f32[2,2,256,256]{3,2,1,0:T(8,128)}, u32[]{:S(2)}, u32[]{:S(2)}) collective-permute-start(f32[2,2,256,256]{3,2,1,0:T(8,128)} %pad_maximum_fusion.7), channel_id=1, source_target_pairs={{0,4},{4,8},{8,12},{12,16},{16,20},{20,24},{24,28},{28,32},{32,36}... | collective-permute-start | bytes 3145736 | tf_op jit(solution)/shard_map/while/body/eval_jaxpr/ppermute | solution.py:26
  736.2 11.4 %collective-permute-start.2 = (f32[1,256]{1,0:T(1,128)S(1)}, f32[1,256]{1,0:T(1,128)S(1)}, u32[]{:S(2)}, u32[]{:S(2)}) collective-permute-start(f32[1,256]{1,0:T(1,128)S(1)} %get-tuple-element.673), channel_id=1, source_target_pairs={{0,4},{4,8},{8,12},{12,16},{16,20},{20,24},{24,28},{28,32},{32,36}... | collective-permute-start | bytes 3080 | tf_op jit(solution)/shard_map/while/body/eval_jaxpr/ppermute | solution.py:17
  737.5 10.2 %collective-permute-start.3 = (f32[1,256]{1,0:T(1,128)S(1)}, f32[1,256]{1,0:T(1,128)S(1)}, u32[]{:S(2)}, u32[]{:S(2)}) collective-permute-start(f32[1,256]{1,0:T(1,128)S(1)} %get-tuple-element.674), channel_id=1, source_target_pairs={{4,0},{8,4},{12,8},{16,12},{20,16},{24,20},{28,24},{32,28},{36,32}... | collective-permute-start | bytes 3080 | tf_op jit(solution)/shard_map/while/body/eval_jaxpr/ppermute | solution.py:18
  748.5 78.4 %all-to-all-start = ((f32[32,8,256]{2,1,0:T(8,128)}), f32[32,8,256]{2,1,0:T(8,128)S(1)}, u32[]{:S(2)}, u32[]{:S(2)}) async-start(f32[32,8,256]{2,1,0:T(8,128)} %stack.9), calls=%async_computation | async-start | bytes 524288 | tf_op jit(solution)/shard_map/while/body/eval_jaxpr/all_to_all | solution.py:117
  (111 other events, 406.7 us)
Sparse Core Ops, SparseCore 0:
  841.7 142.5 all-reduce.12
